TPU v7x, 32 devices: a whole 2x2x4 slice. The times are simulated.
32 devices in a mesh: blk: 2 (over core), leaf: 16 (over z, y, x).
Axes of the slice: x: 2, y: 2, z: 4, core: 2. Of those that a mesh axis runs over, the one named last changes fastest.
Arguments:
- positions: float32 [3, 16, 2, 512], P(None, 'leaf', 'blk'), may hold values from 0 to 32, as said below
- panel_areas: float32 [16, 2, 512], P('leaf', 'blk'), may hold values from 0.5 to 2
- probe_cols: bfloat16 [576, 16, 2, 512], P(None, 'leaf', 'blk'), may hold values from -5 to 5
- full_sketch: bfloat16 [576, 16, 2, 512], P(None, 'leaf', 'blk'), may hold values from -3 to 3
- tree_order: int32 [16, 2, 512], P('leaf', 'blk'), may hold values from 0 to 511, each once within a row
- leaf_basis: bfloat16 [16, 2, 512, 512], P('leaf', 'blk'), may hold values from -0.1875 to 0.1875
- transfer_mats: bfloat16 [16, 3, 512, 512], P('leaf'), may hold values from -0.1875 to 0.1875
Outputs:
- offdiag_sketch: bfloat16 [576, 16, 2, 512], P(None, 'leaf', 'blk')
- nested_sketch: float32 [16, 2, 576, 512], P('leaf')
Inputs may be any that keep to these rules, and one draw needn't show every extreme that they name: `positions`: each leaf's panel centres lie on a surface patch of 32 by 32 mean panel widths. `tree_order`: along the last dimension, each row names every one of the 512 panels of its block once.
All inputs are finite; a program needn't handle non-finite values.
Results may differ from a plain program's by a relative error of at most 0.0046.
Values sent between devices are 32-bit elements; how exact they have to be, the bound alone decides.
A program may use at most 64 MiB of HBM per device.

v0:
```python
import math

import jax
import jax.numpy as jnp
from jax import lax
from jax.sharding import PartitionSpec as P

inv_four_pi = 1.0 / (4.0 * math.pi)


def partner(value, axis, bit):
    mask = 2**bit
    pairs = [(source, source ^ mask) for source in range(lax.axis_size(axis))]
    return lax.ppermute(value, axis, pairs)


def kernel_tile(target_pos, target_area, source_pos, source_area):
    distance = jnp.zeros((target_pos.shape[1], source_pos.shape[1]), jnp.float32)
    for component in range(3):
        gap = target_pos[component][:, None] - source_pos[component][None, :]
        distance = distance + gap * gap
    soft = distance + 0.5 * (target_area[:, None] + source_area[None, :])
    return (inv_four_pi * lax.rsqrt(soft)).astype(jnp.bfloat16)


def target_blocks(target_pos, target_area):
    panels = target_pos.shape[1]
    block_size = min(512, panels)
    block_count = panels // block_size
    pos_blocks = jnp.transpose(target_pos.reshape(3, block_count, block_size), (1, 0, 2))
    return (pos_blocks, target_area.reshape(block_count, block_size))


def near_block(target_pos, target_area, source_pos, source_area, source_scaled):
    pos_blocks, area_blocks = target_blocks(target_pos, target_area)

    def one_block(entry):
        block_pos, block_area = entry
        kernel = kernel_tile(block_pos, block_area, source_pos, source_area)
        return lax.dot_general(
            source_scaled, kernel, (((1,), (1,)), ((), ())), preferred_element_type=jnp.float32
        )

    sums = lax.map(one_block, (pos_blocks, area_blocks))
    return jnp.transpose(sums, (1, 0, 2)).reshape(source_scaled.shape[0], target_pos.shape[1])


def project(current, level_mat):
    return jnp.dot(current, level_mat.astype(jnp.float32), precision=lax.Precision.HIGHEST)


def climb_both(sketch, probes, level_mats):
    for tree_level in range(level_mats.shape[0]):
        sketch_proj = project(sketch, level_mats[tree_level])
        probe_proj = project(probes, level_mats[tree_level])
        other_sketch, other_probe = partner((sketch_proj, probe_proj), "leaf", tree_level)
        sketch = sketch_proj + other_sketch
        probes = probe_proj + other_probe
    return (sketch, probes)


def shards(positions, panel_areas, probe_cols, full_sketch, tree_order, leaf_basis, transfer_mats):
    panels = positions.shape[3]
    probe_count = probe_cols.shape[0]
    basis_width = leaf_basis.shape[3]
    level_count = transfer_mats.shape[1]
    coords = positions.reshape(3, panels)
    area_row = panel_areas.reshape(1, panels)
    probe_flat = probe_cols.reshape(probe_count, panels)
    scaled = (area_row * probe_flat.astype(jnp.float32)).astype(jnp.bfloat16)
    sorting = tree_order.reshape(panels)
    basis_flat = leaf_basis.reshape(panels, basis_width)
    level_mats = transfer_mats.reshape(level_count, basis_width, basis_width)
    probe_part = jnp.dot(
        jnp.take(probe_flat, sorting, axis=1), basis_flat, preferred_element_type=jnp.float32
    )
    outgoing = jnp.concatenate([coords, area_row, scaled.astype(jnp.float32)], axis=0)
    piece = lax.all_gather(outgoing, "blk", axis=1, tiled=True)
    near_sum = near_block(coords, area_row[0], piece[:3], piece[3], piece[4:].astype(jnp.bfloat16))
    offdiag = (full_sketch.reshape(probe_count, panels).astype(jnp.float32) - near_sum).astype(
        jnp.bfloat16
    )
    sketch_part = jnp.dot(
        jnp.take(offdiag, sorting, axis=1), basis_flat, preferred_element_type=jnp.float32
    )
    sketch_sum, probe_sum = lax.psum((sketch_part, probe_part), "blk")
    sketch_top, probe_top = climb_both(sketch_sum, probe_sum, level_mats)
    nested = jnp.stack([sketch_top, probe_top], axis=0)[None]
    return (offdiag.reshape(probe_count, 1, 1, panels), nested)


def solution(mesh):
    in_specs = (
        P(None, "leaf", "blk", None),
        P("leaf", "blk", None),
        P(None, "leaf", "blk", None),
        P(None, "leaf", "blk", None),
        P("leaf", "blk", None),
        P("leaf", "blk", None, None),
        P("leaf", None, None, None),
    )
    out_specs = (P(None, "leaf", "blk", None), P("leaf", None, None, None))
    return jax.shard_map(shards, mesh=mesh, in_specs=in_specs, out_specs=out_specs, check_vma=False)
```

profile of v0, /device:TPU:0, one launch (start us, length us, event | category | flops | bytes accessed | tf_op | source)
XLA Modules:
  0.0 180.8 jit_solution(11477205307398495394)
XLA Ops:
  7.2 1.4 copy.13
  9.2 1.6 pad_maximum_fusion
  10.9 0.6 copy-done.6
  11.5 2.0 %gather_fusion.1 = bf16[512,576]{1,0:T(8,128)(2,1)S(1)} fusion(bf16[576,512]{0,1:T(8,128)(2,1)S(1)} %bitcast.51, s32[1024]{0:T(1024)S(1)} %pad_clamp_fusion), kind=kCustom, calls=%fused_computation.1.clone | custom fusion | bytes 1181696 | tf_op jit(solution)/shard_map/jit(_take)/gather | solution.py:75
  13.5 1.6 fusion.23
  15.2 9.8 %all-gather.2.cloned.1.call-done = f32[580,1024]{0,1:T(8,128)} async-done(((f32[580,512]{0,1:T(8,128)}), f32[580,1024]{0,1:T(8,128)}) %all-gather.2.cloned.1.call-update) | async-done | bytes 2375696 | tf_op jit(solution)/shard_map/all_gather | solution.py:78
  25.0 2.8 %slice_reduce_fusion.3 = (f32[1024]{0:T(1024)S(1)}, f32[1024]{0:T(1024)S(1)}, f32[1024]{0:T(1024)S(1)}, f32[1024]{0:T(1024)S(1)}) fusion(f32[580,1024]{0,1:T(8,128)} %all-gather.2.cloned.1.call-done), kind=kLoop, calls=%fused_computation.45 | loop fusion | bytes 32768 | tf_op jit(solution)/shard_map/while/body/eval_jaxpr/slice | solution.py:20
  27.9 4.4 %fusion.1 = (bf16[576,1,1,512]{3,0,2,1:T(8,128)(2,1)}, f32[576,512]{1,0:T(8,128)S(1)}) fusion(bf16[576,1,1,512]{3,0,2,1:T(8,128)(2,1)S(1)} %copy-done.3, f32[1024]{0:T(1024)S(1)} %get-tuple-element.18, f32[512]{0:T(512)S(1)} %bitcast.55, f32[1024]{0:T(1024)S(1)} %get-tuple-element.19, f32[512]{0:T(512)S(1)} %bitcast.59, f32[1024]{0:T(1024)S(1)} %get-tuple-element.20, ...), kind=kOutput, calls=%fused_computation.10 | convolution fusion | flops 611680256 | bytes 3694592 | tf_op jit(solution)/shard_map/while/body/eval_jaxpr/dot_general | solution.py:40
  32.5 0.3 copy.15
  32.8 2.2 %gather_fusion = bf16[512,576]{1,0:T(8,128)(2,1)S(1)} fusion(bf16[576,512]{0,1:T(8,128)(2,1)S(1)} %copy.15, s32[1024]{0:T(1024)S(1)} %pad_clamp_fusion), kind=kCustom, calls=%fused_computation.clone | custom fusion | bytes 1181696 | tf_op jit(solution)/shard_map/jit(_take)/gather | solution.py:84
  35.0 1.6 fusion.25
  36.7 23.0 %all-reduce.3.cloned.1.call-done = (f32[576,512]{1,0:T(8,128)}, f32[576,512]{1,0:T(8,128)}) async-done(((f32[576,512]{1,0:T(8,128)}, f32[576,512]{1,0:T(8,128)}), (f32[576,512]{1,0:T(8,128)}, f32[576,512]{1,0:T(8,128)})) %all-reduce.3.cloned.1.call-update) | async-done | bytes 2359312 | tf_op jit(solution)/shard_map/psum | solution.py:86
  59.7 2.5 %fusion.35 = f32[576,512]{1,0:T(8,128)S(1)} fusion(f32[576,512]{1,0:T(8,128)} %get-tuple-element.28, bf16[1,3,512,512]{3,2,1,0:T(8,128)(2,1)S(1)} %copy-done.1), kind=kOutput, calls=%fused_computation.50 | convolution fusion | flops 1811939328 | bytes 2883584 | tf_op jit(solution)/shard_map/dot_general | solution.py:49
  62.1 1.8 collective-permute-start.3
  64.0 1.1 fusion.37
  65.0 0.4 collective-permute-start
  65.4 25.6 %collective-permute-done.3 = f32[576,512]{1,0:T(8,128)S(1)} collective-permute-done((f32[576,512]{1,0:T(8,128)S(1)}, f32[576,512]{1,0:T(8,128)S(1)}, u32[]{:S(2)}, u32[]{:S(2)}) %collective-permute-start.3) | collective-permute-done | bytes 1179680 | tf_op jit(solution)/shard_map/ppermute | solution.py:14
  91.0 1.1 fusion.6
  92.1 1.8 collective-permute-start.4
  93.9 21.7 %collective-permute-done = f32[576,512]{1,0:T(8,128)S(1)} collective-permute-done((f32[576,512]{1,0:T(8,128)S(1)}, f32[576,512]{1,0:T(8,128)S(1)}, u32[]{:S(2)}, u32[]{:S(2)}) %collective-permute-start) | collective-permute-done | bytes 1179680 | tf_op jit(solution)/shard_map/ppermute | solution.py:14
  115.7 1.1 fusion.10
  116.8 1.8 %collective-permute-start.1 = (f32[576,512]{1,0:T(8,128)S(1)}, f32[576,512]{1,0:T(8,128)S(1)}, u32[]{:S(2)}, u32[]{:S(2)}) collective-permute-start(f32[576,512]{1,0:T(8,128)S(1)} %fusion.10), channel_id=1, source_target_pairs={{0,2},{1,3},{2,0},{3,1},{4,6},{5,7},{6,4},{7,5},{8,10},{9,11},{10,... | collective-permute-start | bytes 3538952 | tf_op jit(solution)/shard_map/ppermute | solution.py:14
  118.6 0.3 collective-permute-done.4
  118.9 1.1 fusion.4
  120.0 1.8 %collective-permute-start.5 = (f32[576,512]{1,0:T(8,128)S(1)}, f32[576,512]{1,0:T(8,128)S(1)}, u32[]{:S(2)}, u32[]{:S(2)}) collective-permute-start(f32[576,512]{1,0:T(8,128)S(1)} %fusion.4), channel_id=1, source_target_pairs={{0,4},{1,5},{2,6},{3,7},{4,0},{5,1},{6,2},{7,3},{8,12},{9,13},{10,... | collective-permute-start | bytes 3538952 | tf_op jit(solution)/shard_map/ppermute | solution.py:14
  121.9 22.4 %collective-permute-done.1 = f32[576,512]{1,0:T(8,128)S(1)} collective-permute-done((f32[576,512]{1,0:T(8,128)S(1)}, f32[576,512]{1,0:T(8,128)S(1)}, u32[]{:S(2)}, u32[]{:S(2)}) %collective-permute-start.1) | collective-permute-done | bytes 1179680 | tf_op jit(solution)/shard_map/ppermute | solution.py:14
  144.2 1.1 fusion.8
  145.3 1.8 %collective-permute-start.2 = (f32[576,512]{1,0:T(8,128)S(1)}, f32[576,512]{1,0:T(8,128)S(1)}, u32[]{:S(2)}, u32[]{:S(2)}) collective-permute-start(f32[576,512]{1,0:T(8,128)S(1)} %fusion.8), channel_id=1, source_target_pairs={{0,4},{1,5},{2,6},{3,7},{4,0},{5,1},{6,2},{7,3},{8,12},{9,13},{10,... | collective-permute-start | bytes 3538952 | tf_op jit(solution)/shard_map/ppermute | solution.py:14
  147.1 0.2 add_bitcast_fusion
  147.4 24.7 %collective-permute-done.2 = f32[576,512]{1,0:T(8,128)S(1)} collective-permute-done((f32[576,512]{1,0:T(8,128)S(1)}, f32[576,512]{1,0:T(8,128)S(1)}, u32[]{:S(2)}, u32[]{:S(2)}) %collective-permute-start.2) | collective-permute-done | bytes 1179680 | tf_op jit(solution)/shard_map/ppermute | solution.py:14
  172.1 0.2 add_bitcast_fusion.1
  172.4 1.6 maximum_bitcast_fusion
  (26 shorter events, 0.8 us)
Async XLA Ops:
  7.2 6.4 %copy-start = (bf16[1,1,512,512]{3,2,1,0:T(8,128)(2,1)S(1)}, bf16[1,1,512,512]{3,2,1,0:T(8,128)(2,1)}, u32[]{:S(2)}) copy-start(bf16[1,1,512,512]{3,2,1,0:T(8,128)(2,1)} %param.14) | copy-start | bytes 1572868
  7.2 1.5 copy-start.5
  7.2 1.6 copy-start.4
  7.2 17.8 %all-gather.2.cloned.1.call-start = ((), (), s32[]{:S(2)}) async-start(), calls=%async_computation | async-start | bytes 3932160 | tf_op jit(solution)/shard_map/all_gather | solution.py:78
  10.8 0.7 copy-start.6
  10.8 48.9 %all-reduce.3.cloned.1.call-start = ((), (), s32[]{:S(2)}) async-start(), calls=%async_computation.1 | async-start | bytes 4718592 | tf_op jit(solution)/shard_map/psum | solution.py:86
  15.2 12.7 %copy-start.3 = (bf16[576,1,1,512]{3,0,2,1:T(8,128)(2,1)S(1)}, bf16[576,1,1,512]{3,0,2,1:T(8,128)(2,1)}, u32[]{:S(2)}) copy-start(bf16[576,1,1,512]{3,0,2,1:T(8,128)(2,1)} %param.12) | copy-start | bytes 1769476
  36.6 23.0 %copy-start.1 = (bf16[1,3,512,512]{3,2,1,0:T(8,128)(2,1)S(1)}, bf16[1,3,512,512]{3,2,1,0:T(8,128)(2,1)}, u32[]{:S(2)}) copy-start(bf16[1,3,512,512]{3,2,1,0:T(8,128)(2,1)} %param.15) | copy-start | bytes 4718596
  59.7 4.3 %copy-start.2 = (f32[576,512]{1,0:T(8,128)S(1)}, f32[576,512]{1,0:T(8,128)}, u32[]{:S(2)}) copy-start(f32[576,512]{1,0:T(8,128)} %get-tuple-element.29) | copy-start | bytes 3538948
  62.1 28.9 %collective-permute-start.3 = (f32[576,512]{1,0:T(8,128)S(1)}, f32[576,512]{1,0:T(8,128)S(1)}, u32[]{:S(2)}, u32[]{:S(2)}) collective-permute-start(f32[576,512]{1,0:T(8,128)S(1)} %fusion.35), channel_id=1, source_target_pairs={{0,1},{1,0},{2,3},{3,2},{4,5},{5,4},{6,7},{7,6},{8,9},{9,8},{10,11... | collective-permute-start | bytes 3538952 | tf_op jit(solution)/shard_map/ppermute | solution.py:14
  65.0 50.6 %collective-permute-start = (f32[576,512]{1,0:T(8,128)S(1)}, f32[576,512]{1,0:T(8,128)S(1)}, u32[]{:S(2)}, u32[]{:S(2)}) collective-permute-start(f32[576,512]{1,0:T(8,128)S(1)} %fusion.37), channel_id=1, source_target_pairs={{0,1},{1,0},{2,3},{3,2},{4,5},{5,4},{6,7},{7,6},{8,9},{9,8},{10,11... | collective-permute-start | bytes 3538952 | tf_op jit(solution)/shard_map/ppermute | solution.py:14
  92.1 26.8 %collective-permute-start.4 = (f32[576,512]{1,0:T(8,128)S(1)}, f32[576,512]{1,0:T(8,128)S(1)}, u32[]{:S(2)}, u32[]{:S(2)}) collective-permute-start(f32[576,512]{1,0:T(8,128)S(1)} %fusion.6), channel_id=1, source_target_pairs={{0,2},{1,3},{2,0},{3,1},{4,6},{5,7},{6,4},{7,5},{8,10},{9,11},{10,... | collective-permute-start | bytes 3538952 | tf_op jit(solution)/shard_map/ppermute | solution.py:14
  116.8 27.4 %collective-permute-start.1 = (f32[576,512]{1,0:T(8,128)S(1)}, f32[576,512]{1,0:T(8,128)S(1)}, u32[]{:S(2)}, u32[]{:S(2)}) collective-permute-start(f32[576,512]{1,0:T(8,128)S(1)} %fusion.10), channel_id=1, source_target_pairs={{0,2},{1,3},{2,0},{3,1},{4,6},{5,7},{6,4},{7,5},{8,10},{9,11},{10,... | collective-permute-start | bytes 3538952 | tf_op jit(solution)/shard_map/ppermute | solution.py:14
  120.0 27.1 %collective-permute-start.5 = (f32[576,512]{1,0:T(8,128)S(1)}, f32[576,512]{1,0:T(8,128)S(1)}, u32[]{:S(2)}, u32[]{:S(2)}) collective-permute-start(f32[576,512]{1,0:T(8,128)S(1)} %fusion.4), channel_id=1, source_target_pairs={{0,4},{1,5},{2,6},{3,7},{4,0},{5,1},{6,2},{7,3},{8,12},{9,13},{10,... | collective-permute-start | bytes 3538952 | tf_op jit(solution)/shard_map/ppermute | solution.py:14
  145.3 26.8 %collective-permute-start.2 = (f32[576,512]{1,0:T(8,128)S(1)}, f32[576,512]{1,0:T(8,128)S(1)}, u32[]{:S(2)}, u32[]{:S(2)}) collective-permute-start(f32[576,512]{1,0:T(8,128)S(1)} %fusion.8), channel_id=1, source_target_pairs={{0,4},{1,5},{2,6},{3,7},{4,0},{5,1},{6,2},{7,3},{8,12},{9,13},{10,... | collective-permute-start | bytes 3538952 | tf_op jit(solution)/shard_map/ppermute | solution.py:14
Sparse Core Ops, SparseCore 0:
  10.9 14.0 all-gather.1
  36.8 22.8 all-reduce.2
where the time goes:
time: 181 us
  waiting for transfers between devices  128 us (71%)
  matrix products  15.7 us (9%)
  between operations  14.2 us (8%)
  local copies, waits for them, and re-layouts  9.69 us (5%)
  starting transfers between devices  9.49 us (5%)
  other arithmetic  4.1 us (2%)
    ppermute x6, waiting for transfers between devices, partner(): return lax.ppermute(value, axis, pairs)  94.8 us
    psum x1, waiting for transfers between devices, shards(): sketch_sum, probe_sum = lax.psum((sketch_part, probe_part), 'blk')  23 us
    all_gather x1, waiting for transfers between devices, shards(): piece = lax.all_gather(outgoing, 'blk', axis=1, tiled=True)  9.85 us
    ppermute x6, starting transfers between devices, partner(): return lax.ppermute(value, axis, pairs)  9.41 us
    dot_general x6, matrix products, project(): jnp.dot(current, level_mat.astype(jnp.float32), precision=lax.Precision.H...  7.97 us
    dot_general x1, matrix products, one_block(): lax.dot_general(source_scaled, kernel, (((1,), (1,)), ((), ())), preferre...  4.45 us
  transfers between devices with their start and end apart: 8, of which 7 were waited for; matrix products, arithmetic and copies ran while one was open for 5% of the time, Pallas kernels for 0%

commit v1 on v0

v1 whole, which is shorter than its diff:
```python
import functools
import math

import jax
import jax.numpy as jnp
from jax import lax
from jax.experimental import pallas as pl
from jax.experimental.pallas import tpu as pltpu
from jax.sharding import PartitionSpec as P

MESH = pl.DeviceIdType.MESH
inv_four_pi = 1.0 / (4.0 * math.pi)


def chunk_rows(share):
    return max(rows for rows in range(8, min(share, 72) + 1, 8) if share % rows == 0)


def leaf_partner(me, level):
    step = 2**level
    return me + step * (1 - 2 * lax.rem(lax.div(me, step), 2))


def kernel(
    blocks, levels, chunk,
    pos_ref, area_ref, order_ref, probe_hbm, full_hbm, basis_hbm, mats_hbm,
    off_hbm, nested_hbm,
    probe, full, basis, mats, sorted_basis, tile, geo, geo_in, columns, scaled, scaled_in,
    near, off, part, part_in, going, coming, done,
    load_sem, off_sem, geo_send, geo_recv, scaled_send, scaled_recv, part_send, part_recv,
    level_send, level_recv, done_send, done_recv, done_local,
):
    count, panels = probe.shape
    share = count // blocks
    per_half = share // chunk
    total = 2 * per_half
    my_blk = lax.axis_index("blk")
    my_leaf = lax.axis_index("leaf")
    peers = [lax.rem(my_blk + distance, blocks) for distance in range(1, blocks)]
    partners = [leaf_partner(my_leaf, level) for level in range(levels)]

    loads = [
        pltpu.make_async_copy(source, target, load_sem.at[index])
        for index, (source, target) in enumerate(
            [(probe_hbm, probe), (basis_hbm, basis), (mats_hbm, mats), (full_hbm, full)]
        )
    ]
    for load in loads:
        load.start()

    barrier = pltpu.get_barrier_semaphore()
    for peer in peers:
        pl.semaphore_signal(barrier, inc=1, device_id={"blk": peer}, device_id_type=MESH)
    for partner in partners:
        pl.semaphore_signal(barrier, inc=1, device_id={"leaf": partner}, device_id_type=MESH)

    def to_peers(source, target, send, recv):
        return [
            pltpu.make_async_remote_copy(
                src_ref=source, dst_ref=target.at[index], send_sem=send.at[index],
                recv_sem=recv.at[index], device_id={"blk": peer}, device_id_type=MESH,
            )
            for index, peer in enumerate(peers)
        ]

    def rows_of_peer(half):
        return [
            pltpu.make_async_remote_copy(
                src_ref=part.at[half, pl.ds(pl.multiple_of(peer * share, 8), share)],
                dst_ref=part_in.at[half, index],
                send_sem=part_send.at[half, index], recv_sem=part_recv.at[half, index],
                device_id={"blk": peer}, device_id_type=MESH,
            )
            for index, peer in enumerate(peers)
        ]

    geo_copies = to_peers(geo, geo_in, geo_send, geo_recv)
    scaled_copies = to_peers(scaled, scaled_in, scaled_send, scaled_recv)
    part_copies = [rows_of_peer(0), rows_of_peer(1)]

    def chunk_slice(position):
        return pl.ds(pl.multiple_of(position * chunk, 8), chunk)

    def exchange(level, position):
        rows = chunk_slice(position)
        return pltpu.make_async_remote_copy(
            src_ref=going.at[level, rows], dst_ref=coming.at[level, rows],
            send_sem=level_send.at[level, position], recv_sem=level_recv.at[level, position],
            device_id={"leaf": partners[level]}, device_id_type=MESH,
        )

    def result_rows(position):
        half = 1 - lax.div(position, per_half)
        start = my_blk * share + lax.rem(position, per_half) * chunk
        return nested_hbm.at[0, half, pl.ds(pl.multiple_of(start, 8), chunk)]

    def result_copies(position):
        return [
            pltpu.make_async_remote_copy(
                src_ref=done.at[chunk_slice(position)], dst_ref=result_rows(position),
                send_sem=done_send.at[index, position], recv_sem=done_recv.at[index, position],
                device_id={"blk": peer}, device_id_type=MESH,
            )
            for index, peer in enumerate(peers)
        ]

    def local_result(position):
        return pltpu.make_async_copy(
            done.at[chunk_slice(position)], result_rows(position), done_local.at[position]
        )

    def project(value, level):
        high = value.astype(jnp.bfloat16).astype(jnp.float32)
        both = jnp.concatenate([high, value - high], axis=0).astype(jnp.bfloat16)
        product = jnp.dot(both, mats[level], preferred_element_type=jnp.float32)
        return product[:chunk] + product[chunk:]

    def first_level(half, inner):
        start = pl.multiple_of(my_blk * share + inner * chunk, 8)
        value = part[half, pl.ds(start, chunk), :]
        for index in range(blocks - 1):
            value = value + part_in[half, index, chunk_slice(inner), :]
        position = half * per_half + inner
        going[0, chunk_slice(position), :] = project(value, 0)
        exchange(0, position).start()

    def joined(level, position):
        exchange(level, position).wait_recv()
        rows = chunk_slice(position)
        return going[level, rows, :] + coming[level, rows, :]

    def next_level(level, position):
        going[level, chunk_slice(position), :] = project(joined(level - 1, position), level)
        exchange(level, position).start()

    def finish(position):
        done[chunk_slice(position), :] = joined(levels - 1, position)
        for copy in result_copies(position):
            copy.start()
        local_result(position).start()

    def kernel_tile(source):
        step = min(128, panels)

        def some_rows(index, carry):
            rows = pl.ds(pl.multiple_of(index * step, step), step)
            values = columns[rows, :]
            distance = jnp.zeros((step, panels), jnp.float32)
            for component in range(3):
                gap = geo[component : component + 1, :] - values[:, component : component + 1]
                distance = distance + gap * gap
            soft = distance + 0.5 * (geo[3:4, :] + values[:, 3:4])
            tile[rows, :] = (inv_four_pi * lax.rsqrt(soft)).astype(jnp.bfloat16)
            return carry

        columns[...] = jnp.transpose(source)
        lax.fori_loop(0, panels // step, some_rows, 0)

    geo[...] = jnp.zeros_like(geo)
    geo[0:3, :] = pos_ref[...]
    geo[3:4, :] = area_ref[...]
    places = lax.broadcasted_iota(jnp.int32, (panels, panels), 0)
    chosen = jnp.where(places == order_ref[...], 1.0, 0.0).astype(jnp.bfloat16)
    loads[1].wait()
    sorted_basis[...] = jnp.dot(
        chosen, basis[...], preferred_element_type=jnp.float32
    ).astype(jnp.bfloat16)
    loads[0].wait()
    part[0] = jnp.dot(probe[...], sorted_basis[...], preferred_element_type=jnp.float32)
    pl.semaphore_wait(barrier, blocks - 1 + levels)
    for copy in part_copies[0] + geo_copies:
        copy.start()
    scaled[...] = (
        (area_ref[...] * probe[...].astype(jnp.float32)).astype(jnp.bfloat16).astype(jnp.float32)
    )
    for copy in scaled_copies:
        copy.start()
    kernel_tile(geo[...])
    loads[2].wait()
    for copy in part_copies[0]:
        copy.wait_recv()

    def first_probe(inner, carry):
        first_level(0, inner)
        return carry

    lax.fori_loop(0, per_half, first_probe, 0)
    near[...] = jnp.dot(
        scaled[...].astype(jnp.bfloat16), tile[...], preferred_element_type=jnp.float32
    )
    for index in range(blocks - 1):
        geo_copies[index].wait_recv()
        kernel_tile(geo_in[index])
        scaled_copies[index].wait_recv()
        near[...] += jnp.dot(
            scaled_in[index].astype(jnp.bfloat16), tile[...], preferred_element_type=jnp.float32
        )
    loads[3].wait()
    off[...] = (full[...].astype(jnp.float32) - near[...]).astype(jnp.bfloat16)
    off_copy = pltpu.make_async_copy(off, off_hbm, off_sem.at[0])
    off_copy.start()
    if per_half > 2:
        next_level(1, 0)
    part[1] = jnp.dot(off[...], sorted_basis[...], preferred_element_type=jnp.float32)
    for copy in part_copies[1]:
        copy.start()
    for position in range(1, per_half - 2):
        next_level(1, position)
    for position in range(per_half - 3):
        next_level(2, position)
    for position in range(per_half - 4):
        finish(position)
    for copy in part_copies[1]:
        copy.wait_recv()

    def one_step(step, carry):
        @pl.when(step < total)
        def _():
            first_level(1, step - per_half)

        for level in range(1, levels):
            @pl.when((step >= level + 1) & (step < total + level + 1))
            def _(level=level):
                next_level(level, step - level - 1)

        @pl.when((step >= levels + 1) & (step < total + levels + 1))
        def _():
            finish(step - levels - 1)

        return carry

    lax.fori_loop(per_half, total + levels + 1, one_step, 0)

    def settle(position, carry):
        for level in range(levels):
            exchange(level, position).wait_send()
        for copy in result_copies(position):
            copy.wait()
        local_result(position).wait()
        return carry

    lax.fori_loop(0, total, settle, 0)
    off_copy.wait()
    for copy in geo_copies + scaled_copies + part_copies[0] + part_copies[1]:
        copy.wait_send()


def shards(positions, panel_areas, probe_cols, full_sketch, tree_order, leaf_basis, transfer_mats):
    panels = positions.shape[3]
    count = probe_cols.shape[0]
    width = leaf_basis.shape[3]
    levels = transfer_mats.shape[1]
    blocks = lax.axis_size("blk")
    share = count // blocks
    chunk = chunk_rows(share)
    total = 2 * share // chunk
    f32, b16 = jnp.float32, jnp.bfloat16
    dma = pltpu.SemaphoreType.DMA
    whole = pl.BlockSpec(memory_space=pltpu.VMEM)
    anywhere = pl.BlockSpec(memory_space=pl.ANY)
    offdiag, nested = pl.pallas_call(
        functools.partial(kernel, blocks, levels, chunk),
        out_shape=(
            jax.ShapeDtypeStruct((count, panels), b16),
            jax.ShapeDtypeStruct((1, 2, count, width), f32),
        ),
        in_specs=[whole] * 3 + [anywhere] * 4,
        out_specs=(anywhere, anywhere),
        scratch_shapes=[
            pltpu.VMEM((count, panels), b16),
            pltpu.VMEM((count, panels), b16),
            pltpu.VMEM((panels, width), b16),
            pltpu.VMEM((levels, width, width), b16),
            pltpu.VMEM((panels, width), b16),
            pltpu.VMEM((panels, panels), b16),
            pltpu.VMEM((8, panels), f32),
            pltpu.VMEM((blocks - 1, 8, panels), f32),
            pltpu.VMEM((panels, 8), f32),
            pltpu.VMEM((count, panels), f32),
            pltpu.VMEM((blocks - 1, count, panels), f32),
            pltpu.VMEM((count, panels), f32),
            pltpu.VMEM((count, panels), b16),
            pltpu.VMEM((2, count, width), f32),
            pltpu.VMEM((2, blocks - 1, share, width), f32),
            pltpu.VMEM((levels, 2 * share, width), f32),
            pltpu.VMEM((levels, 2 * share, width), f32),
            pltpu.VMEM((2 * share, width), f32),
            dma((4,)), dma((1,)),
            dma((blocks - 1,)), dma((blocks - 1,)),
            dma((blocks - 1,)), dma((blocks - 1,)),
            dma((2, blocks - 1)), dma((2, blocks - 1)),
            dma((levels, total)), dma((levels, total)),
            dma((blocks - 1, total)), dma((blocks - 1, total)),
            dma((total,)),
        ],
        compiler_params=pltpu.CompilerParams(
            collective_id=0, has_side_effects=True, vmem_limit_bytes=48 * 2**20
        ),
    )(
        positions.reshape(3, panels),
        panel_areas.reshape(1, panels),
        tree_order.reshape(1, panels),
        probe_cols.reshape(count, panels),
        full_sketch.reshape(count, panels),
        leaf_basis.reshape(panels, width),
        transfer_mats.reshape(levels, width, width),
    )
    return (offdiag.reshape(count, 1, 1, panels), nested)


def solution(mesh):
    in_specs = (
        P(None, "leaf", "blk", None),
        P("leaf", "blk", None),
        P(None, "leaf", "blk", None),
        P(None, "leaf", "blk", None),
        P("leaf", "blk", None),
        P("leaf", "blk", None, None),
        P("leaf", None, None, None),
    )
    out_specs = (P(None, "leaf", "blk", None), P("leaf", None, None, None))
    return jax.shard_map(shards, mesh=mesh, in_specs=in_specs, out_specs=out_specs, check_vma=False)
```

time: 181 us -> 59.2 us (0.33)
  waiting for transfers between devices: 128 us -> 0 us
  Pallas kernels: 0 us -> 47.4 us
  matrix products: 15.7 us -> 0 us
  between operations: 14.2 us -> 0.64 us
  starting transfers between devices: 9.49 us -> 0 us
  other arithmetic: 4.1 us -> 0 us
    ppermute x6 -> x0, waiting for transfers between devices: 94.8 us -> none  [partner(): return lax.ppermute(value, axis, pairs)]
    pallas_call x0 -> x1, Pallas kernels: none -> 47.4 us  [shards(): pl.pallas_call(functools.partial(kernel, blocks, levels, chunk), out_shap...]
    psum x1 -> x0, waiting for transfers between devices: 23 us -> none  [shards(): sketch_sum, probe_sum = lax.psum((sketch_part, probe_part), 'blk')]
    dot_general x9 -> x0, matrix products: 15.7 us -> none  [the longest x6 7.97 us: project(): jnp.dot(current, level_mat.astype(jnp.float32), precision=lax.Precision.H...]
    all_gather x1 -> x0, waiting for transfers between devices: 9.85 us -> none  [shards(): piece = lax.all_gather(outgoing, 'blk', axis=1, tiled=True)]
    ppermute x6 -> x0, starting transfers between devices: 9.41 us -> none  [partner(): return lax.ppermute(value, axis, pairs)]
    unnamed x16 -> x15, local copies, waits for them, and re-layouts: 2.18 us -> 10.7 us
    gather x2 -> x0, local copies, waits for them, and re-layouts: 4.23 us -> none  [the longest x1 2.2 us: shards(): jnp.take(offdiag, sorting, axis=1)]
  transfers between devices with their start and end apart: 8 -> 0, of which waited for: 7 -> 0; matrix products, arithmetic and copies ran while one was open for 5% -> 0% of each run, Pallas kernels for 0% -> 0%
where the time goes in v1:
time: 59.2 us; the launch traced here: 58.8 us
  Pallas kernels  47.4 us (80%)
  local copies, waits for them, and re-layouts  10.7 us (18%)
  between operations  0.64 us (1%)
    pallas_call x1, Pallas kernels, shards(): pl.pallas_call(functools.partial(kernel, blocks, levels, chunk), out_shap...  47.4 us
    unnamed x15, local copies, waits for them, and re-layouts  10.7 us

profile of v1, /device:TPU:0, one launch (start us, length us, event | category | flops | bytes accessed | tf_op | source)
XLA Modules:
  0.0 58.8 jit_solution(10713753396328555967)
XLA Ops:
  0.6 0.7 %copy.11 = f32[3,1,1,512]{3,0,1,2:T(4,128)S(1)} copy(f32[3,1,1,512]{3,2,1,0:T(1,128)} %param.7) | data formatting | bytes 12288
  1.3 0.0 copy-start
  1.3 1.4 %copy-done = bf16[1,3,512,512]{3,2,1,0:T(8,128)(2,1)S(1)} copy-done((bf16[1,3,512,512]{3,2,1,0:T(8,128)(2,1)S(1)}, bf16[1,3,512,512]{3,2,1,0:T(8,128)(2,1)}, u32[]{:S(2)}) %copy-start) | copy-done | bytes 1572888
  2.7 0.0 copy-start.1
  2.7 1.1 %copy-done.1 = bf16[576,1,1,512]{3,0,2,1:T(8,128)(2,1)S(1)} copy-done((bf16[576,1,1,512]{3,0,2,1:T(8,128)(2,1)S(1)}, bf16[576,1,1,512]{3,0,2,1:T(8,128)(2,1)}, u32[]{:S(2)}) %copy-start.1) | copy-done | bytes 589848
  3.8 0.0 copy-start.2
  3.8 1.1 %copy-done.2 = bf16[576,1,1,512]{3,0,2,1:T(8,128)(2,1)S(1)} copy-done((bf16[576,1,1,512]{3,0,2,1:T(8,128)(2,1)S(1)}, bf16[576,1,1,512]{3,0,2,1:T(8,128)(2,1)}, u32[]{:S(2)}) %copy-start.2) | copy-done | bytes 589848
  4.9 0.0 copy-start.3
  4.9 1.0 %copy-done.3 = bf16[1,1,512,512]{3,2,1,0:T(8,128)(2,1)S(1)} copy-done((bf16[1,1,512,512]{3,2,1,0:T(8,128)(2,1)S(1)}, bf16[1,1,512,512]{3,2,1,0:T(8,128)(2,1)}, u32[]{:S(2)}) %copy-start.3) | copy-done | bytes 524312
  5.9 0.0 copy-start.4
  5.9 0.7 %copy-done.4 = f32[1,1,512]{2,1,0:T(1,128)S(1)} copy-done((f32[1,1,512]{2,1,0:T(1,128)S(1)}, f32[1,1,512]{2,1,0:T(1,128)}, u32[]{:S(2)}) %copy-start.4) | copy-done | bytes 2072
  6.6 0.0 copy-start.5
  6.6 0.7 %copy-done.5 = s32[1,1,512]{2,1,0:T(1,128)S(1)} copy-done((s32[1,1,512]{2,1,0:T(1,128)S(1)}, s32[1,1,512]{2,1,0:T(1,128)}, u32[]{:S(2)}) %copy-start.5) | copy-done | bytes 2072
  7.3 47.4 %shard_map.86 = (bf16[576,512]{1,0:T(8,128)(2,1)S(1)}, f32[1,2,576,512]{3,2,1,0:T(8,128)}) custom-call(f32[3,512]{1,0:T(4,128)S(1)} %bitcast.15, f32[1,512]{1,0:T(1,128)S(1)} %bitcast.16, s32[1,512]{1,0:T(1,128)S(1)} %bitcast.17, bf16[576,512]{1,0:T(8,128)(2,1)S(1)} %bitcast.11, bf16[576,512]{1,0:T(8,128)(2,1)S(1)} %bitcast.12, ...), custom_call_target="tpu_custom_call" | custom-call | tf_op jit(solution)/shard_map/pallas_call | solution.py:261
  54.7 0.8 %copy.14 = bf16[576,1,1,512]{3,0,2,1:T(8,128)(2,1)} copy(bf16[576,1,1,512]{3,0,2,1:T(8,128)(2,1)S(1)} %bitcast.13) | data formatting | bytes 1179648
  55.5 3.3 %copy.15 = f32[1,2,576,512]{3,2,1,0:T(8,128)} copy(f32[1,2,576,512]{3,2,1,0:T(8,128)} %get-tuple-element.9) | data formatting | bytes 4718592
Async XLA Ops:
  1.3 1.4 %copy-start = (bf16[1,3,512,512]{3,2,1,0:T(8,128)(2,1)S(1)}, bf16[1,3,512,512]{3,2,1,0:T(8,128)(2,1)}, u32[]{:S(2)}) copy-start(bf16[1,3,512,512]{3,2,1,0:T(8,128)(2,1)} %param.13) | copy-start | bytes 4718596
  2.7 1.1 %copy-start.1 = (bf16[576,1,1,512]{3,0,2,1:T(8,128)(2,1)S(1)}, bf16[576,1,1,512]{3,0,2,1:T(8,128)(2,1)}, u32[]{:S(2)}) copy-start(bf16[576,1,1,512]{3,0,2,1:T(8,128)(2,1)} %param.9) | copy-start | bytes 1769476
  3.8 1.1 %copy-start.2 = (bf16[576,1,1,512]{3,0,2,1:T(8,128)(2,1)S(1)}, bf16[576,1,1,512]{3,0,2,1:T(8,128)(2,1)}, u32[]{:S(2)}) copy-start(bf16[576,1,1,512]{3,0,2,1:T(8,128)(2,1)} %param.10) | copy-start | bytes 1769476
  4.9 1.0 %copy-start.3 = (bf16[1,1,512,512]{3,2,1,0:T(8,128)(2,1)S(1)}, bf16[1,1,512,512]{3,2,1,0:T(8,128)(2,1)}, u32[]{:S(2)}) copy-start(bf16[1,1,512,512]{3,2,1,0:T(8,128)(2,1)} %param.12) | copy-start | bytes 1572868
  5.9 0.7 %copy-start.4 = (f32[1,1,512]{2,1,0:T(1,128)S(1)}, f32[1,1,512]{2,1,0:T(1,128)}, u32[]{:S(2)}) copy-start(f32[1,1,512]{2,1,0:T(1,128)} %param.8) | copy-start | bytes 6148
  6.6 0.7 %copy-start.5 = (s32[1,1,512]{2,1,0:T(1,128)S(1)}, s32[1,1,512]{2,1,0:T(1,128)}, u32[]{:S(2)}) copy-start(s32[1,1,512]{2,1,0:T(1,128)} %param.11) | copy-start | bytes 6148

commit v2 on v1

v2 whole, which is shorter than its diff:
```python
import functools
import math

import jax
import jax.numpy as jnp
from jax import lax
from jax.experimental import pallas as pl
from jax.experimental.pallas import tpu as pltpu
from jax.sharding import PartitionSpec as P

MESH = pl.DeviceIdType.MESH
inv_four_pi = 1.0 / (4.0 * math.pi)


def chunk_rows(share):
    return max(rows for rows in range(8, min(share, 48) + 1, 8) if share % rows == 0)


def leaf_partner(me, level):
    step = 2**level
    return me + step * (1 - 2 * lax.rem(lax.div(me, step), 2))


def kernel(
    blocks, levels, chunk,
    pos_hbm, area_hbm, order_hbm, probe_hbm, full_hbm, basis_hbm, mats_hbm,
    off, nested,
    order, probe, full, basis, mats, sorted_basis, tile, geo, geo_in, columns, scaled, scaled_in,
    near, part, part_in, going, coming,
    load_sem, geo_send, geo_recv, scaled_send, scaled_recv, part_send, part_recv,
    level_send, level_recv, done_send, done_recv,
):
    count, panels = probe.shape
    share = count // blocks
    per_half = share // chunk
    total = 2 * per_half
    my_blk = lax.axis_index("blk")
    my_leaf = lax.axis_index("leaf")
    peers = [lax.rem(my_blk + distance, blocks) for distance in range(1, blocks)]
    partners = [leaf_partner(my_leaf, level) for level in range(levels)]

    loads = [
        pltpu.make_async_copy(source, target, load_sem.at[index])
        for index, (source, target) in enumerate(
            [
                (order_hbm.at[0], order), (basis_hbm, basis), (probe_hbm, probe),
                (area_hbm.at[0], geo.at[pl.ds(3, 1)]),
            ]
            + [(pos_hbm.at[axis, 0], geo.at[pl.ds(axis, 1)]) for axis in range(3)]
            + [(mats_hbm, mats), (full_hbm, full)]
        )
    ]
    order_load, basis_load, probe_load, *geo_loads, mats_load, full_load = loads
    geo[...] = jnp.zeros_like(geo)
    for load in loads:
        load.start()

    barrier = pltpu.get_barrier_semaphore()
    for peer in peers:
        pl.semaphore_signal(barrier, inc=1, device_id={"blk": peer}, device_id_type=MESH)
    for partner in partners:
        pl.semaphore_signal(barrier, inc=1, device_id={"leaf": partner}, device_id_type=MESH)

    def to_peers(source, target, send, recv):
        return [
            pltpu.make_async_remote_copy(
                src_ref=source, dst_ref=target.at[index], send_sem=send.at[index],
                recv_sem=recv.at[index], device_id={"blk": peer}, device_id_type=MESH,
            )
            for index, peer in enumerate(peers)
        ]

    def part_copies(half, inner):
        start, size = (0, share) if inner is None else (inner * chunk, chunk)
        place = 0 if inner is None else inner
        return [
            pltpu.make_async_remote_copy(
                src_ref=part.at[half, pl.ds(pl.multiple_of(peer * share + start, 8), size)],
                dst_ref=part_in.at[half, index, pl.ds(pl.multiple_of(start, 8), size)],
                send_sem=part_send.at[half, index],
                recv_sem=part_recv.at[half, index, place],
                device_id={"blk": peer}, device_id_type=MESH,
            )
            for index, peer in enumerate(peers)
        ]

    geo_copies = to_peers(geo, geo_in, geo_send, geo_recv)
    scaled_copies = to_peers(scaled, scaled_in, scaled_send, scaled_recv)

    def chunk_slice(position):
        return pl.ds(pl.multiple_of(position * chunk, 8), chunk)

    def exchange(level, position):
        rows = chunk_slice(position)
        return pltpu.make_async_remote_copy(
            src_ref=going.at[level, rows], dst_ref=coming.at[level, rows],
            send_sem=level_send.at[level], recv_sem=level_recv.at[level, position],
            device_id={"leaf": partners[level]}, device_id_type=MESH,
        )

    def result_copies(half, rows):
        return [
            pltpu.make_async_remote_copy(
                src_ref=nested.at[0, 1 - half, rows], dst_ref=nested.at[0, 1 - half, rows],
                send_sem=done_send.at[half, index], recv_sem=done_recv.at[half, index],
                device_id={"blk": peer}, device_id_type=MESH,
            )
            for index, peer in enumerate(peers)
        ]

    def project(value, level):
        high = value.astype(jnp.bfloat16).astype(jnp.float32)
        both = jnp.concatenate([high, value - high], axis=0).astype(jnp.bfloat16)
        product = jnp.dot(both, mats[level], preferred_element_type=jnp.float32)
        return product[:chunk] + product[chunk:]

    def first_level(half, inner):
        for copy in part_copies(half, inner):
            copy.wait_recv()
        start = pl.multiple_of(my_blk * share + inner * chunk, 8)
        value = part[half, pl.ds(start, chunk), :]
        for index in range(blocks - 1):
            value = value + part_in[half, index, chunk_slice(inner), :]
        position = half * per_half + inner
        going[0, chunk_slice(position), :] = project(value, 0)
        exchange(0, position).start()

    def joined(level, position):
        exchange(level, position).wait_recv()
        rows = chunk_slice(position)
        return going[level, rows, :] + coming[level, rows, :]

    def next_level(level, position):
        going[level, chunk_slice(position), :] = project(joined(level - 1, position), level)
        exchange(level, position).start()

    def finish(position):
        half = lax.div(position, per_half)
        start = my_blk * share + lax.rem(position, per_half) * chunk
        rows = pl.ds(pl.multiple_of(start, 8), chunk)
        nested[0, 1 - half, rows, :] = joined(levels - 1, position)
        for copy in result_copies(half, rows):
            copy.start()

    def kernel_tile(source):
        step = min(128, panels)

        def some_rows(index, carry):
            rows = pl.ds(pl.multiple_of(index * step, step), step)
            values = columns[rows, :]
            distance = jnp.zeros((step, panels), jnp.float32)
            for component in range(3):
                gap = geo[component : component + 1, :] - values[:, component : component + 1]
                distance = distance + gap * gap
            soft = distance + 0.5 * (geo[3:4, :] + values[:, 3:4])
            tile[rows, :] = (inv_four_pi * lax.rsqrt(soft)).astype(jnp.bfloat16)
            return carry

        columns[...] = jnp.transpose(source)
        lax.fori_loop(0, panels // step, some_rows, 0)

    def send_part(half):
        def one(inner, carry):
            for copy in part_copies(half, inner):
                copy.start()
            return carry

        lax.fori_loop(0, per_half, one, 0)

    order_load.wait()
    places = lax.broadcasted_iota(jnp.int32, (panels, panels), 0)
    chosen = jnp.where(places == order[...], 1.0, 0.0).astype(jnp.bfloat16)
    basis_load.wait()
    sorted_basis[...] = jnp.dot(
        chosen, basis[...], preferred_element_type=jnp.float32
    ).astype(jnp.bfloat16)
    probe_load.wait()
    part[0] = jnp.dot(probe[...], sorted_basis[...], preferred_element_type=jnp.float32)
    pl.semaphore_wait(barrier, blocks - 1 + levels)
    send_part(0)
    for load in geo_loads:
        load.wait()
    scaled[...] = (
        (geo[3:4, :] * probe[...].astype(jnp.float32)).astype(jnp.bfloat16).astype(jnp.float32)
    )
    for copy in geo_copies + scaled_copies:
        copy.start()
    mats_load.wait()

    def first_probe(inner, carry):
        first_level(0, inner)
        return carry

    lax.fori_loop(0, per_half, first_probe, 0)
    kernel_tile(geo[...])
    near[...] = jnp.dot(
        scaled[...].astype(jnp.bfloat16), tile[...], preferred_element_type=jnp.float32
    )
    if per_half > 2:
        next_level(1, 0)
    for index in range(blocks - 1):
        geo_copies[index].wait_recv()
        kernel_tile(geo_in[index])
        scaled_copies[index].wait_recv()
        near[...] += jnp.dot(
            scaled_in[index].astype(jnp.bfloat16), tile[...], preferred_element_type=jnp.float32
        )
    full_load.wait()
    off[...] = (full[...].astype(jnp.float32) - near[...]).astype(jnp.bfloat16)
    part[1] = jnp.dot(off[...], sorted_basis[...], preferred_element_type=jnp.float32)
    send_part(1)
    for position in range(1, per_half - 2):
        next_level(1, position)
        for level in range(2, levels):
            if position >= 2 * level - 2:
                next_level(level, position - 2 * level + 2)

    def one_step(step, carry):
        @pl.when(step < total)
        def _():
            first_level(1, step - per_half)

        for level in range(1, levels):
            @pl.when((step >= 2 * level) & (step < total + 2 * level))
            def _(level=level):
                next_level(level, step - 2 * level)

        @pl.when((step >= 2 * levels) & (step < total + 2 * levels))
        def _():
            finish(step - 2 * levels)

        return carry

    lax.fori_loop(per_half, total + 2 * levels, one_step, 0)
    for level in range(levels):
        pltpu.make_async_remote_copy(
            src_ref=going.at[level], dst_ref=coming.at[level],
            send_sem=level_send.at[level], recv_sem=level_recv.at[level, 0],
            device_id={"leaf": partners[level]}, device_id_type=MESH,
        ).wait_send()
    for half in range(2):
        for copy in result_copies(half, pl.ds(0, share)):
            copy.wait()
        for copy in part_copies(half, None):
            copy.wait_send()
    for copy in geo_copies + scaled_copies:
        copy.wait_send()


def shards(positions, panel_areas, probe_cols, full_sketch, tree_order, leaf_basis, transfer_mats):
    panels = positions.shape[3]
    count = probe_cols.shape[0]
    width = leaf_basis.shape[3]
    levels = transfer_mats.shape[1]
    blocks = lax.axis_size("blk")
    share = count // blocks
    chunk = chunk_rows(share)
    total = 2 * share // chunk
    f32, b16 = jnp.float32, jnp.bfloat16
    dma = pltpu.SemaphoreType.DMA
    whole = pl.BlockSpec(memory_space=pltpu.VMEM)
    hbm = pl.BlockSpec(memory_space=pltpu.HBM)
    offdiag, nested = pl.pallas_call(
        functools.partial(kernel, blocks, levels, chunk),
        out_shape=(
            pltpu.VMEM((count, panels), b16),
            pltpu.VMEM((1, 2, count, width), f32),
        ),
        in_specs=[hbm] * 7,
        out_specs=(whole, whole),
        scratch_shapes=[
            pltpu.VMEM((1, panels), jnp.int32),
            pltpu.VMEM((count, panels), b16),
            pltpu.VMEM((count, panels), b16),
            pltpu.VMEM((panels, width), b16),
            pltpu.VMEM((levels, width, width), b16),
            pltpu.VMEM((panels, width), b16),
            pltpu.VMEM((panels, panels), b16),
            pltpu.VMEM((8, panels), f32),
            pltpu.VMEM((blocks - 1, 8, panels), f32),
            pltpu.VMEM((panels, 8), f32),
            pltpu.VMEM((count, panels), f32),
            pltpu.VMEM((blocks - 1, count, panels), f32),
            pltpu.VMEM((count, panels), f32),
            pltpu.VMEM((2, count, width), f32),
            pltpu.VMEM((2, blocks - 1, share, width), f32),
            pltpu.VMEM((levels, 2 * share, width), f32),
            pltpu.VMEM((levels, 2 * share, width), f32),
            dma((9,)),
            dma((blocks - 1,)), dma((blocks - 1,)),
            dma((blocks - 1,)), dma((blocks - 1,)),
            dma((2, blocks - 1)), dma((2, blocks - 1, total // 2)),
            dma((levels,)), dma((levels, total)),
            dma((2, blocks - 1)), dma((2, blocks - 1)),
        ],
        compiler_params=pltpu.CompilerParams(
            collective_id=0, has_side_effects=True, vmem_limit_bytes=58 * 2**20
        ),
    )(
        positions,
        panel_areas,
        tree_order,
        probe_cols.reshape(count, panels),
        full_sketch.reshape(count, panels),
        leaf_basis.reshape(panels, width),
        transfer_mats.reshape(levels, width, width),
    )
    return (offdiag.reshape(count, 1, 1, panels), nested)


def solution(mesh):
    in_specs = (
        P(None, "leaf", "blk", None),
        P("leaf", "blk", None),
        P(None, "leaf", "blk", None),
        P(None, "leaf", "blk", None),
        P("leaf", "blk", None),
        P("leaf", "blk", None, None),
        P("leaf", None, None, None),
    )
    out_specs = (P(None, "leaf", "blk", None), P("leaf", None, None, None))
    return jax.shard_map(shards, mesh=mesh, in_specs=in_specs, out_specs=out_specs, check_vma=False)
```

time: 59.2 us -> 46.5 us (0.79)
  local copies, waits for them, and re-layouts: 10.7 us -> 2.22 us
  Pallas kernels: 47.4 us -> 43.5 us
    unnamed x15 -> x2, local copies, waits for them, and re-layouts: 10.7 us -> 2.22 us
    pallas_call x1, Pallas kernels: 47.4 us -> 43.5 us  [shards(): pl.pallas_call(functools.partial(kernel, blocks, levels, chunk), out_shap...]
where the time goes in v2:
time: 46.5 us; the launch traced here: 46.4 us
  Pallas kernels  43.5 us (94%)
  local copies, waits for them, and re-layouts  2.22 us (5%)
  between operations  0.64 us (1%)
    pallas_call x1, Pallas kernels, shards(): pl.pallas_call(functools.partial(kernel, blocks, levels, chunk), out_shap...  43.5 us
    unnamed x2, local copies, waits for them, and re-layouts  2.22 us

profile of v2, /device:TPU:0, one launch (start us, length us, event | category | flops | bytes accessed | tf_op | source)
XLA Modules:
  0.0 46.4 jit_solution(1737787678176663969)
XLA Ops:
  0.6 43.5 %shard_map.86 = (bf16[576,512]{1,0:T(8,128)(2,1)S(1)}, f32[1,2,576,512]{3,2,1,0:T(8,128)S(1)}) custom-call(f32[3,1,1,512]{3,2,1,0:T(1,128)} %pos_hbm.1, f32[1,1,512]{2,1,0:T(1,128)} %area_hbm.1, s32[1,1,512]{2,1,0:T(1,128)} %order_hbm.1, bf16[576,512]{1,0:T(8,128)(2,1)} %bitcast.7, bf16[576,512]{1,0:T(8,128)(2,1)} %bitcast.8, bf16[512,512]{1,0:T(8,128)(2,1)} %bitcast.9, ...), custom_call_target="tpu_custom_call" | custom-call | tf_op jit(solution)/shard_map/pallas_call | solution.py:263
  44.2 0.8 %copy.11 = bf16[576,1,1,512]{3,0,2,1:T(8,128)(2,1)} copy(bf16[576,1,1,512]{3,0,2,1:T(8,128)(2,1)S(1)} %bitcast.5) | data formatting | bytes 1179648
  45.0 1.4 %copy.12 = f32[1,2,576,512]{3,2,1,0:T(8,128)} copy(f32[1,2,576,512]{3,2,1,0:T(8,128)S(1)} %get-tuple-element.7) | data formatting | bytes 4718592

commit v3 on v2

--- a/solution.py
+++ b/solution.py
@@ -13,7 +13,7 @@
 
 
 def chunk_rows(share):
-    return max(rows for rows in range(8, min(share, 48) + 1, 8) if share % rows == 0)
+    return max(rows for rows in range(8, min(share, 32) + 1, 8) if share % rows == 0)
 
 
 def leaf_partner(me, level):
@@ -51,15 +51,14 @@
         )
     ]
     order_load, basis_load, probe_load, *geo_loads, mats_load, full_load = loads
-    geo[...] = jnp.zeros_like(geo)
-    for load in loads:
-        load.start()
-
     barrier = pltpu.get_barrier_semaphore()
     for peer in peers:
         pl.semaphore_signal(barrier, inc=1, device_id={"blk": peer}, device_id_type=MESH)
     for partner in partners:
         pl.semaphore_signal(barrier, inc=1, device_id={"leaf": partner}, device_id_type=MESH)
+    geo[...] = jnp.zeros_like(geo)
+    for load in [order_load, basis_load, probe_load] + geo_loads:
+        load.start()
 
     def to_peers(source, target, send, recv):
         return [
@@ -159,6 +158,23 @@
         columns[...] = jnp.transpose(source)
         lax.fori_loop(0, panels // step, some_rows, 0)
 
+    def project_part(half, source, barrier=None):
+        def some(rows):
+            part[half, rows, :] = jnp.dot(
+                source[rows, :], sorted_basis[...], preferred_element_type=jnp.float32
+            )
+
+        if share % 16 == 0:
+            for peer in peers:
+                some(pl.ds(pl.multiple_of(peer * share, 16), share))
+        else:
+            some(pl.ds(0, count))
+        if barrier is not None:
+            pl.semaphore_wait(barrier, blocks - 1 + levels)
+        send_part(half)
+        if share % 16 == 0:
+            some(pl.ds(pl.multiple_of(my_blk * share, 16), share))
+
     def send_part(half):
         def one(inner, carry):
             for copy in part_copies(half, inner):
@@ -167,17 +183,36 @@
 
         lax.fori_loop(0, per_half, one, 0)
 
+    def one_step(step):
+        @pl.when((step >= per_half) & (step < total))
+        def _():
+            first_level(1, step - per_half)
+
+        for level in range(1, levels):
+            @pl.when((step >= 2 * level) & (step < total + 2 * level))
+            def _(level=level):
+                next_level(level, step - 2 * level)
+
+        @pl.when((step >= 2 * levels) & (step < total + 2 * levels))
+        def _():
+            finish(step - 2 * levels)
+
+    early = min(per_half, 5)
+
+    def early_step(step):
+        if step < early:
+            one_step(step)
+
     order_load.wait()
     places = lax.broadcasted_iota(jnp.int32, (panels, panels), 0)
     chosen = jnp.where(places == order[...], 1.0, 0.0).astype(jnp.bfloat16)
     basis_load.wait()
+    mats_load.start()
     sorted_basis[...] = jnp.dot(
         chosen, basis[...], preferred_element_type=jnp.float32
     ).astype(jnp.bfloat16)
     probe_load.wait()
-    part[0] = jnp.dot(probe[...], sorted_basis[...], preferred_element_type=jnp.float32)
-    pl.semaphore_wait(barrier, blocks - 1 + levels)
-    send_part(0)
+    project_part(0, probe, barrier)
     for load in geo_loads:
         load.wait()
     scaled[...] = (
@@ -186,6 +221,7 @@
     for copy in geo_copies + scaled_copies:
         copy.start()
     mats_load.wait()
+    full_load.start()
 
     def first_probe(inner, carry):
         first_level(0, inner)
@@ -196,42 +232,21 @@
     near[...] = jnp.dot(
         scaled[...].astype(jnp.bfloat16), tile[...], preferred_element_type=jnp.float32
     )
-    if per_half > 2:
-        next_level(1, 0)
+    early_step(2)
     for index in range(blocks - 1):
         geo_copies[index].wait_recv()
         kernel_tile(geo_in[index])
+        if index == blocks - 2:
+            early_step(3)
         scaled_copies[index].wait_recv()
         near[...] += jnp.dot(
             scaled_in[index].astype(jnp.bfloat16), tile[...], preferred_element_type=jnp.float32
         )
     full_load.wait()
     off[...] = (full[...].astype(jnp.float32) - near[...]).astype(jnp.bfloat16)
-    part[1] = jnp.dot(off[...], sorted_basis[...], preferred_element_type=jnp.float32)
-    send_part(1)
-    for position in range(1, per_half - 2):
-        next_level(1, position)
-        for level in range(2, levels):
-            if position >= 2 * level - 2:
-                next_level(level, position - 2 * level + 2)
-
-    def one_step(step, carry):
-        @pl.when(step < total)
-        def _():
-            first_level(1, step - per_half)
-
-        for level in range(1, levels):
-            @pl.when((step >= 2 * level) & (step < total + 2 * level))
-            def _(level=level):
-                next_level(level, step - 2 * level)
-
-        @pl.when((step >= 2 * levels) & (step < total + 2 * levels))
-        def _():
-            finish(step - 2 * levels)
-
-        return carry
-
-    lax.fori_loop(per_half, total + 2 * levels, one_step, 0)
+    early_step(4)
+    project_part(1, off)
+    lax.fori_loop(early, total + 2 * levels, lambda step, carry: one_step(step), None)
     for level in range(levels):
         pltpu.make_async_remote_copy(
             src_ref=going.at[level], dst_ref=coming.at[level],
@@ -245,6 +260,24 @@
             copy.wait_send()
     for copy in geo_copies + scaled_copies:
         copy.wait_send()
+
+
+def write_out(pieces, off, nested, off_hbm, nested_hbm, sem):
+    rows = nested.shape[2] // pieces
+    copies = [
+        pltpu.make_async_copy(
+            nested.at[0, half, pl.ds(piece * rows, rows)],
+            nested_hbm.at[0, half, pl.ds(piece * rows, rows)],
+            sem.at[half * pieces + piece],
+        )
+        for half in range(2)
+        for piece in range(pieces)
+    ]
+    copies.append(pltpu.make_async_copy(off, off_hbm, sem.at[2 * pieces]))
+    for copy in copies:
+        copy.start()
+    for copy in copies:
+        copy.wait()
 
 
 def shards(positions, panel_areas, probe_cols, full_sketch, tree_order, leaf_basis, transfer_mats):
@@ -305,6 +338,18 @@
         leaf_basis.reshape(panels, width),
         transfer_mats.reshape(levels, width, width),
     )
+    pieces = 4
+    offdiag, nested = pl.pallas_call(
+        functools.partial(write_out, pieces),
+        out_shape=(
+            jax.ShapeDtypeStruct((count, panels), b16),
+            jax.ShapeDtypeStruct((1, 2, count, width), f32),
+        ),
+        in_specs=(whole, whole),
+        out_specs=(hbm, hbm),
+        scratch_shapes=[dma((1 + 2 * pieces,))],
+        compiler_params=pltpu.CompilerParams(vmem_limit_bytes=2**20),
+    )(offdiag, nested)
     return (offdiag.reshape(count, 1, 1, panels), nested)
 
 

time: 46.5 us -> 47.7 us (1.026)
  Pallas kernels: 43.5 us -> 46.8 us
  local copies, waits for them, and re-layouts: 2.22 us -> 0 us
    unnamed x2 -> x0, local copies, waits for them, and re-layouts: 2.22 us -> none
    pallas_call x0 -> x1, Pallas kernels: none -> 1.67 us  [shards(): pl.pallas_call(functools.partial(write_out, pieces), out_shape=(jax.Shape...]
    pallas_call x1, Pallas kernels: 43.5 us -> 45.2 us  [shards(): pl.pallas_call(functools.partial(kernel, blocks, levels, chunk), out_shap...]
where the time goes in v3:
time: 47.7 us; the launch traced here: 47.5 us
  Pallas kernels  46.8 us (98%)
  between operations  0.64 us (1%)
    pallas_call x1, Pallas kernels, shards(): pl.pallas_call(functools.partial(kernel, blocks, levels, chunk), out_shap...  45.2 us
    pallas_call x1, Pallas kernels, shards(): pl.pallas_call(functools.partial(write_out, pieces), out_shape=(jax.Shape...  1.67 us

profile of v3, /device:TPU:0, one launch (start us, length us, event | category | flops | bytes accessed | tf_op | source)
XLA Modules:
  0.0 47.5 jit_solution(15469571970416214120)
XLA Ops:
  0.6 45.2 %shard_map.86 = (bf16[576,512]{1,0:T(8,128)(2,1)S(1)}, f32[1,2,576,512]{3,2,1,0:T(8,128)S(1)}) custom-call(f32[3,1,1,512]{3,2,1,0:T(1,128)} %pos_hbm.1, f32[1,1,512]{2,1,0:T(1,128)} %area_hbm.1, s32[1,1,512]{2,1,0:T(1,128)} %order_hbm.1, bf16[576,512]{1,0:T(8,128)(2,1)} %bitcast.6, bf16[576,512]{1,0:T(8,128)(2,1)} %bitcast.7, bf16[512,512]{1,0:T(8,128)(2,1)} %bitcast.8, ...), custom_call_target="tpu_custom_call" | custom-call | tf_op jit(solution)/shard_map/pallas_call | solution.py:296
  45.8 1.7 %shard_map.87 = (bf16[576,512]{1,0:T(8,128)(2,1)}, f32[1,2,576,512]{3,2,1,0:T(8,128)}) custom-call(bf16[576,512]{1,0:T(8,128)(2,1)S(1)} %get-tuple-element.6.off, f32[1,2,576,512]{3,2,1,0:T(8,128)S(1)} %get-tuple-element.7.nested), custom_call_target="tpu_custom_call" | custom-call | tf_op jit(solution)/shard_map/pallas_call | solution.py:342

commit v4 on v3

--- a/solution.py
+++ b/solution.py
@@ -33,6 +33,7 @@
     count, panels = probe.shape
     share = count // blocks
     per_half = share // chunk
+    lag = 3
     total = 2 * per_half
     my_blk = lax.axis_index("blk")
     my_leaf = lax.axis_index("leaf")
@@ -69,15 +70,13 @@
             for index, peer in enumerate(peers)
         ]
 
-    def part_copies(half, inner):
-        start, size = (0, share) if inner is None else (inner * chunk, chunk)
-        place = 0 if inner is None else inner
+    def part_copies(half, start, size):
         return [
             pltpu.make_async_remote_copy(
                 src_ref=part.at[half, pl.ds(pl.multiple_of(peer * share + start, 8), size)],
-                dst_ref=part_in.at[half, index, pl.ds(pl.multiple_of(start, 8), size)],
+                dst_ref=part_in.at[half, index, pl.ds(start, size)],
                 send_sem=part_send.at[half, index],
-                recv_sem=part_recv.at[half, index, place],
+                recv_sem=part_recv.at[half, index, min(start, 1)],
                 device_id={"blk": peer}, device_id_type=MESH,
             )
             for index, peer in enumerate(peers)
@@ -108,38 +107,71 @@
         ]
 
     def project(value, level):
+        rows = value.shape[0]
         high = value.astype(jnp.bfloat16).astype(jnp.float32)
         both = jnp.concatenate([high, value - high], axis=0).astype(jnp.bfloat16)
         product = jnp.dot(both, mats[level], preferred_element_type=jnp.float32)
-        return product[:chunk] + product[chunk:]
-
-    def first_level(half, inner):
-        for copy in part_copies(half, inner):
+        return product[:rows] + product[rows:]
+
+    def first_level(half, start, size):
+        for copy in part_copies(half, start, size):
             copy.wait_recv()
-        start = pl.multiple_of(my_blk * share + inner * chunk, 8)
-        value = part[half, pl.ds(start, chunk), :]
+        mine = pl.multiple_of(my_blk * share + start, 8)
+        value = part[half, pl.ds(mine, size), :]
         for index in range(blocks - 1):
-            value = value + part_in[half, index, chunk_slice(inner), :]
-        position = half * per_half + inner
-        going[0, chunk_slice(position), :] = project(value, 0)
-        exchange(0, position).start()
-
-    def joined(level, position):
-        exchange(level, position).wait_recv()
-        rows = chunk_slice(position)
-        return going[level, rows, :] + coming[level, rows, :]
-
-    def next_level(level, position):
-        going[level, chunk_slice(position), :] = project(joined(level - 1, position), level)
-        exchange(level, position).start()
-
-    def finish(position):
-        half = lax.div(position, per_half)
-        start = my_blk * share + lax.rem(position, per_half) * chunk
-        rows = pl.ds(pl.multiple_of(start, 8), chunk)
-        nested[0, 1 - half, rows, :] = joined(levels - 1, position)
-        for copy in result_copies(half, rows):
-            copy.start()
+            value = value + part_in[half, index, pl.ds(start, size), :]
+        going[0, pl.ds(half * share + start, size), :] = project(value, 0)
+
+        def send(position, carry):
+            exchange(0, position).start()
+            return carry
+
+        first = (half * share + start) // chunk
+        lax.fori_loop(first, first + size // chunk, send, 0)
+
+    def one_step(step, active):
+        for level, on in enumerate(active):
+            if on:
+                exchange(level, step - lag * level).wait_recv()
+        values = [
+            going[level, chunk_slice(step - lag * level), :]
+            + coming[level, chunk_slice(step - lag * level), :]
+            for level in range(levels)
+            if active[level]
+        ]
+        results = [
+            project(value, level + 1) if level < levels - 1 else value
+            for value, level in zip(values, [level for level in range(levels) if active[level]])
+        ]
+        for result, level in zip(results, [level for level in range(levels) if active[level]]):
+            position = step - lag * level
+            if level < levels - 1:
+                going[level + 1, chunk_slice(position), :] = result
+                exchange(level + 1, position).start()
+            else:
+                half = lax.div(position, per_half)
+                start = my_blk * share + lax.rem(position, per_half) * chunk
+                rows = pl.ds(pl.multiple_of(start, 8), chunk)
+                nested[0, 1 - half, rows, :] = result
+                for copy in result_copies(half, rows):
+                    copy.start()
+
+    def steps(start, stop):
+        edges = sorted({lag * level for level in range(levels)})
+        edges = sorted(set(edges + [edge + total for edge in edges] + [start, stop]))
+        for low, high in zip(edges, edges[1:]):
+            if low < start or high > stop:
+                continue
+            active = [lag * level <= low < total + lag * level for level in range(levels)]
+            if high - low <= 1:
+                one_step(low, active)
+            else:
+
+                def body(step, carry, active=active):
+                    one_step(step, active)
+                    return carry
+
+                lax.fori_loop(low, high, body, 0)
 
     def kernel_tile(source):
         step = min(128, panels)
@@ -158,7 +190,7 @@
         columns[...] = jnp.transpose(source)
         lax.fori_loop(0, panels // step, some_rows, 0)
 
-    def project_part(half, source, barrier=None):
+    def project_part(half, source, sizes, barrier=None):
         def some(rows):
             part[half, rows, :] = jnp.dot(
                 source[rows, :], sorted_basis[...], preferred_element_type=jnp.float32
@@ -171,37 +203,18 @@
             some(pl.ds(0, count))
         if barrier is not None:
             pl.semaphore_wait(barrier, blocks - 1 + levels)
-        send_part(half)
+        for start, size in sizes:
+            for copy in part_copies(half, start, size):
+                copy.start()
         if share % 16 == 0:
             some(pl.ds(pl.multiple_of(my_blk * share, 16), share))
 
-    def send_part(half):
-        def one(inner, carry):
-            for copy in part_copies(half, inner):
-                copy.start()
-            return carry
-
-        lax.fori_loop(0, per_half, one, 0)
-
-    def one_step(step):
-        @pl.when((step >= per_half) & (step < total))
-        def _():
-            first_level(1, step - per_half)
-
-        for level in range(1, levels):
-            @pl.when((step >= 2 * level) & (step < total + 2 * level))
-            def _(level=level):
-                next_level(level, step - 2 * level)
-
-        @pl.when((step >= 2 * levels) & (step < total + 2 * levels))
-        def _():
-            finish(step - 2 * levels)
-
-    early = min(per_half, 5)
+    early = min(per_half, 3)
+    probe_sizes = [(0, chunk)] + ([(chunk, share - chunk)] if share > chunk else [])
 
     def early_step(step):
         if step < early:
-            one_step(step)
+            steps(step, step + 1)
 
     order_load.wait()
     places = lax.broadcasted_iota(jnp.int32, (panels, panels), 0)
@@ -212,7 +225,7 @@
         chosen, basis[...], preferred_element_type=jnp.float32
     ).astype(jnp.bfloat16)
     probe_load.wait()
-    project_part(0, probe, barrier)
+    project_part(0, probe, probe_sizes, barrier)
     for load in geo_loads:
         load.wait()
     scaled[...] = (
@@ -223,30 +236,28 @@
     mats_load.wait()
     full_load.start()
 
-    def first_probe(inner, carry):
-        first_level(0, inner)
-        return carry
-
-    lax.fori_loop(0, per_half, first_probe, 0)
+    for start, size in probe_sizes:
+        first_level(0, start, size)
     kernel_tile(geo[...])
     near[...] = jnp.dot(
         scaled[...].astype(jnp.bfloat16), tile[...], preferred_element_type=jnp.float32
     )
-    early_step(2)
+    early_step(0)
     for index in range(blocks - 1):
         geo_copies[index].wait_recv()
         kernel_tile(geo_in[index])
         if index == blocks - 2:
-            early_step(3)
+            early_step(1)
         scaled_copies[index].wait_recv()
         near[...] += jnp.dot(
             scaled_in[index].astype(jnp.bfloat16), tile[...], preferred_element_type=jnp.float32
         )
     full_load.wait()
     off[...] = (full[...].astype(jnp.float32) - near[...]).astype(jnp.bfloat16)
-    early_step(4)
-    project_part(1, off)
-    lax.fori_loop(early, total + 2 * levels, lambda step, carry: one_step(step), None)
+    project_part(1, off, [(0, share)])
+    early_step(2)
+    first_level(1, 0, share)
+    steps(early, total + lag * (levels - 1))
     for level in range(levels):
         pltpu.make_async_remote_copy(
             src_ref=going.at[level], dst_ref=coming.at[level],
@@ -256,7 +267,7 @@
     for half in range(2):
         for copy in result_copies(half, pl.ds(0, share)):
             copy.wait()
-        for copy in part_copies(half, None):
+        for copy in part_copies(half, 0, share):
             copy.wait_send()
     for copy in geo_copies + scaled_copies:
         copy.wait_send()
@@ -322,7 +333,7 @@
             dma((9,)),
             dma((blocks - 1,)), dma((blocks - 1,)),
             dma((blocks - 1,)), dma((blocks - 1,)),
-            dma((2, blocks - 1)), dma((2, blocks - 1, total // 2)),
+            dma((2, blocks - 1)), dma((2, blocks - 1, 2)),
             dma((levels,)), dma((levels, total)),
             dma((2, blocks - 1)), dma((2, blocks - 1)),
         ],

time: 47.7 us -> 45.8 us (0.960)
  Pallas kernels: 46.8 us -> 45 us
    pallas_call x1, Pallas kernels: 45.2 us -> 43.3 us  [shards(): pl.pallas_call(functools.partial(kernel, blocks, levels, chunk), out_shap...]
where the time goes in v4:
time: 45.8 us; the launch traced here: 45.6 us
  Pallas kernels  45 us (98%)
  between operations  0.64 us (1%)
    pallas_call x1, Pallas kernels, shards(): pl.pallas_call(functools.partial(kernel, blocks, levels, chunk), out_shap...  43.3 us
    pallas_call x1, Pallas kernels, shards(): pl.pallas_call(functools.partial(write_out, pieces), out_shape=(jax.Shape...  1.67 us

profile of v4, /device:TPU:0, one launch (start us, length us, event | category | flops | bytes accessed | tf_op | source)
XLA Modules:
  0.0 45.6 jit_solution(10130294286235448460)
XLA Ops:
  0.6 43.3 %shard_map.86 = (bf16[576,512]{1,0:T(8,128)(2,1)S(1)}, f32[1,2,576,512]{3,2,1,0:T(8,128)S(1)}) custom-call(f32[3,1,1,512]{3,2,1,0:T(1,128)} %pos_hbm.1, f32[1,1,512]{2,1,0:T(1,128)} %area_hbm.1, s32[1,1,512]{2,1,0:T(1,128)} %order_hbm.1, bf16[576,512]{1,0:T(8,128)(2,1)} %bitcast.6, bf16[576,512]{1,0:T(8,128)(2,1)} %bitcast.7, bf16[512,512]{1,0:T(8,128)(2,1)} %bitcast.8, ...), custom_call_target="tpu_custom_call" | custom-call | tf_op jit(solution)/shard_map/pallas_call | solution.py:307
  44.0 1.7 %shard_map.87 = (bf16[576,512]{1,0:T(8,128)(2,1)}, f32[1,2,576,512]{3,2,1,0:T(8,128)}) custom-call(bf16[576,512]{1,0:T(8,128)(2,1)S(1)} %get-tuple-element.6.off, f32[1,2,576,512]{3,2,1,0:T(8,128)S(1)} %get-tuple-element.7.nested), custom_call_target="tpu_custom_call" | custom-call | tf_op jit(solution)/shard_map/pallas_call | solution.py:353

commit v5 on v4

--- a/solution.py
+++ b/solution.py
@@ -70,13 +70,13 @@
             for index, peer in enumerate(peers)
         ]
 
-    def part_copies(half, start, size):
+    def part_copies(half, start, size, place=0):
         return [
             pltpu.make_async_remote_copy(
                 src_ref=part.at[half, pl.ds(pl.multiple_of(peer * share + start, 8), size)],
                 dst_ref=part_in.at[half, index, pl.ds(start, size)],
                 send_sem=part_send.at[half, index],
-                recv_sem=part_recv.at[half, index, min(start, 1)],
+                recv_sem=part_recv.at[half, index, place],
                 device_id={"blk": peer}, device_id_type=MESH,
             )
             for index, peer in enumerate(peers)
@@ -113,8 +113,8 @@
         product = jnp.dot(both, mats[level], preferred_element_type=jnp.float32)
         return product[:rows] + product[rows:]
 
-    def first_level(half, start, size):
-        for copy in part_copies(half, start, size):
+    def first_level(half, start, size, place):
+        for copy in part_copies(half, start, size, place):
             copy.wait_recv()
         mine = pl.multiple_of(my_blk * share + start, 8)
         value = part[half, pl.ds(mine, size), :]
@@ -203,14 +203,24 @@
             some(pl.ds(0, count))
         if barrier is not None:
             pl.semaphore_wait(barrier, blocks - 1 + levels)
-        for start, size in sizes:
-            for copy in part_copies(half, start, size):
+        for piece in sizes:
+            for copy in part_copies(half, *piece):
                 copy.start()
         if share % 16 == 0:
             some(pl.ds(pl.multiple_of(my_blk * share, 16), share))
 
     early = min(per_half, 3)
-    probe_sizes = [(0, chunk)] + ([(chunk, share - chunk)] if share > chunk else [])
+
+    def pieces(chunks):
+        found, start = [], 0
+        for size in [rows * chunk for rows in chunks] + [share]:
+            size = min(size, share - start)
+            if size > 0:
+                found.append((start, size, len(found)))
+                start += size
+        return found
+
+    probe_sizes, sketch_sizes = pieces([1, 2, 3]), pieces([3])
 
     def early_step(step):
         if step < early:
@@ -236,8 +246,8 @@
     mats_load.wait()
     full_load.start()
 
-    for start, size in probe_sizes:
-        first_level(0, start, size)
+    for piece in probe_sizes:
+        first_level(0, *piece)
     kernel_tile(geo[...])
     near[...] = jnp.dot(
         scaled[...].astype(jnp.bfloat16), tile[...], preferred_element_type=jnp.float32
@@ -254,9 +264,10 @@
         )
     full_load.wait()
     off[...] = (full[...].astype(jnp.float32) - near[...]).astype(jnp.bfloat16)
-    project_part(1, off, [(0, share)])
+    project_part(1, off, sketch_sizes)
     early_step(2)
-    first_level(1, 0, share)
+    for piece in sketch_sizes:
+        first_level(1, *piece)
     steps(early, total + lag * (levels - 1))
     for level in range(levels):
         pltpu.make_async_remote_copy(
@@ -333,7 +344,7 @@
             dma((9,)),
             dma((blocks - 1,)), dma((blocks - 1,)),
             dma((blocks - 1,)), dma((blocks - 1,)),
-            dma((2, blocks - 1)), dma((2, blocks - 1, 2)),
+            dma((2, blocks - 1)), dma((2, blocks - 1, 4)),
             dma((levels,)), dma((levels, total)),
             dma((2, blocks - 1)), dma((2, blocks - 1)),
         ],

time: 45.8 us -> 45.7 us (level)
  no operation moved by 1% of the time
where the time goes in v5:
time: 45.7 us; the launch traced here: 45.5 us
  Pallas kernels  44.9 us (98%)
  between operations  0.64 us (1%)
    pallas_call x1, Pallas kernels, shards(): pl.pallas_call(functools.partial(kernel, blocks, levels, chunk), out_shap...  43.2 us
    pallas_call x1, Pallas kernels, shards(): pl.pallas_call(functools.partial(write_out, pieces), out_shape=(jax.Shape...  1.67 us

profile of v5, /device:TPU:0, one launch (start us, length us, event | category | flops | bytes accessed | tf_op | source)
XLA Modules:
  0.0 45.5 jit_solution(9440649425585876102)
XLA Ops:
  0.6 43.2 %shard_map.86 = (bf16[576,512]{1,0:T(8,128)(2,1)S(1)}, f32[1,2,576,512]{3,2,1,0:T(8,128)S(1)}) custom-call(f32[3,1,1,512]{3,2,1,0:T(1,128)} %pos_hbm.1, f32[1,1,512]{2,1,0:T(1,128)} %area_hbm.1, s32[1,1,512]{2,1,0:T(1,128)} %order_hbm.1, bf16[576,512]{1,0:T(8,128)(2,1)} %bitcast.6, bf16[576,512]{1,0:T(8,128)(2,1)} %bitcast.7, bf16[512,512]{1,0:T(8,128)(2,1)} %bitcast.8, ...), custom_call_target="tpu_custom_call" | custom-call | tf_op jit(solution)/shard_map/pallas_call | solution.py:318
  43.9 1.7 %shard_map.87 = (bf16[576,512]{1,0:T(8,128)(2,1)}, f32[1,2,576,512]{3,2,1,0:T(8,128)}) custom-call(bf16[576,512]{1,0:T(8,128)(2,1)S(1)} %get-tuple-element.6.off, f32[1,2,576,512]{3,2,1,0:T(8,128)S(1)} %get-tuple-element.7.nested), custom_call_target="tpu_custom_call" | custom-call | tf_op jit(solution)/shard_map/pallas_call | solution.py:364

commit v6 on v5

--- a/solution.py
+++ b/solution.py
@@ -209,8 +209,6 @@
         if share % 16 == 0:
             some(pl.ds(pl.multiple_of(my_blk * share, 16), share))
 
-    early = min(per_half, 3)
-
     def pieces(chunks):
         found, start = [], 0
         for size in [rows * chunk for rows in chunks] + [share]:
@@ -221,10 +219,6 @@
         return found
 
     probe_sizes, sketch_sizes = pieces([1, 2, 3]), pieces([3])
-
-    def early_step(step):
-        if step < early:
-            steps(step, step + 1)
 
     order_load.wait()
     places = lax.broadcasted_iota(jnp.int32, (panels, panels), 0)
@@ -248,26 +242,34 @@
 
     for piece in probe_sizes:
         first_level(0, *piece)
-    kernel_tile(geo[...])
-    near[...] = jnp.dot(
-        scaled[...].astype(jnp.bfloat16), tile[...], preferred_element_type=jnp.float32
-    )
-    early_step(0)
-    for index in range(blocks - 1):
+    def own_near():
+        near[...] = jnp.dot(
+            scaled[...].astype(jnp.bfloat16), tile[...], preferred_element_type=jnp.float32
+        )
+
+    def peer_tile(index):
         geo_copies[index].wait_recv()
         kernel_tile(geo_in[index])
-        if index == blocks - 2:
-            early_step(1)
+
+    def peer_near(index):
         scaled_copies[index].wait_recv()
         near[...] += jnp.dot(
             scaled_in[index].astype(jnp.bfloat16), tile[...], preferred_element_type=jnp.float32
         )
-    full_load.wait()
-    off[...] = (full[...].astype(jnp.float32) - near[...]).astype(jnp.bfloat16)
-    project_part(1, off, sketch_sizes)
-    early_step(2)
-    for piece in sketch_sizes:
-        first_level(1, *piece)
+        if index == blocks - 2:
+            full_load.wait()
+            off[...] = (full[...].astype(jnp.float32) - near[...]).astype(jnp.bfloat16)
+
+    tasks = [lambda: kernel_tile(geo[...]), own_near]
+    for index in range(blocks - 1):
+        tasks += [functools.partial(peer_tile, index), functools.partial(peer_near, index)]
+    tasks.append(lambda: project_part(1, off, sketch_sizes))
+    tasks += [functools.partial(first_level, 1, *piece) for piece in sketch_sizes]
+    early = min(len(tasks) - 1, per_half)
+    for step, task in enumerate(tasks):
+        task()
+        if step < early:
+            steps(step, step + 1)
     steps(early, total + lag * (levels - 1))
     for level in range(levels):
         pltpu.make_async_remote_copy(

time: 45.7 us -> 45 us (0.985)
  Pallas kernels: 44.9 us -> 44.2 us
    pallas_call x1, Pallas kernels: 43.2 us -> 42.5 us  [shards(): pl.pallas_call(functools.partial(kernel, blocks, levels, chunk), out_shap...]
where the time goes in v6:
time: 45 us; the launch traced here: 44.9 us
  Pallas kernels  44.2 us (98%)
  between operations  0.64 us (1%)
    pallas_call x1, Pallas kernels, shards(): pl.pallas_call(functools.partial(kernel, blocks, levels, chunk), out_shap...  42.5 us
    pallas_call x1, Pallas kernels, shards(): pl.pallas_call(functools.partial(write_out, pieces), out_shape=(jax.Shape...  1.67 us

profile of v6, /device:TPU:0, one launch (start us, length us, event | category | flops | bytes accessed | tf_op | source)
XLA Modules:
  0.0 44.9 jit_solution(11825939592503542051)
XLA Ops:
  0.6 42.5 %shard_map.86 = (bf16[576,512]{1,0:T(8,128)(2,1)S(1)}, f32[1,2,576,512]{3,2,1,0:T(8,128)S(1)}) custom-call(f32[3,1,1,512]{3,2,1,0:T(1,128)} %pos_hbm.1, f32[1,1,512]{2,1,0:T(1,128)} %area_hbm.1, s32[1,1,512]{2,1,0:T(1,128)} %order_hbm.1, bf16[576,512]{1,0:T(8,128)(2,1)} %bitcast.6, bf16[576,512]{1,0:T(8,128)(2,1)} %bitcast.7, bf16[512,512]{1,0:T(8,128)(2,1)} %bitcast.8, ...), custom_call_target="tpu_custom_call" | custom-call | tf_op jit(solution)/shard_map/pallas_call | solution.py:320
  43.2 1.7 %shard_map.87 = (bf16[576,512]{1,0:T(8,128)(2,1)}, f32[1,2,576,512]{3,2,1,0:T(8,128)}) custom-call(bf16[576,512]{1,0:T(8,128)(2,1)S(1)} %get-tuple-element.6.off, f32[1,2,576,512]{3,2,1,0:T(8,128)S(1)} %get-tuple-element.7.nested), custom_call_target="tpu_custom_call" | custom-call | tf_op jit(solution)/shard_map/pallas_call | solution.py:366

commit v7 on v6

--- a/solution.py
+++ b/solution.py
@@ -13,7 +13,7 @@
 
 
 def chunk_rows(share):
-    return max(rows for rows in range(8, min(share, 32) + 1, 8) if share % rows == 0)
+    return max(rows for rows in range(8, min(share, 48) + 1, 8) if share % rows == 0)
 
 
 def leaf_partner(me, level):
@@ -33,7 +33,7 @@
     count, panels = probe.shape
     share = count // blocks
     per_half = share // chunk
-    lag = 3
+    lag = 2
     total = 2 * per_half
     my_blk = lax.axis_index("blk")
     my_leaf = lax.axis_index("leaf")
@@ -218,7 +218,7 @@
                 start += size
         return found
 
-    probe_sizes, sketch_sizes = pieces([1, 2, 3]), pieces([3])
+    probe_sizes, sketch_sizes = pieces([1, 2, 3]), pieces([2])
 
     order_load.wait()
     places = lax.broadcasted_iota(jnp.int32, (panels, panels), 0)
@@ -260,9 +260,16 @@
             full_load.wait()
             off[...] = (full[...].astype(jnp.float32) - near[...]).astype(jnp.bfloat16)
 
-    tasks = [lambda: kernel_tile(geo[...]), own_near]
-    for index in range(blocks - 1):
-        tasks += [functools.partial(peer_tile, index), functools.partial(peer_near, index)]
+    def own_block():
+        kernel_tile(geo[...])
+        own_near()
+
+    def peer_block(index):
+        peer_tile(index)
+        peer_near(index)
+
+    tasks = [own_block]
+    tasks += [functools.partial(peer_block, index) for index in range(blocks - 1)]
     tasks.append(lambda: project_part(1, off, sketch_sizes))
     tasks += [functools.partial(first_level, 1, *piece) for piece in sketch_sizes]
     early = min(len(tasks) - 1, per_half)

time: 45 us -> 47 us (1.044)
  Pallas kernels: 44.2 us -> 46.2 us
    pallas_call x1, Pallas kernels: 42.5 us -> 44.5 us  [shards(): pl.pallas_call(functools.partial(kernel, blocks, levels, chunk), out_shap...]
where the time goes in v7:
time: 47 us; the launch traced here: 46.8 us
  Pallas kernels  46.2 us (98%)
  between operations  0.64 us (1%)
    pallas_call x1, Pallas kernels, shards(): pl.pallas_call(functools.partial(kernel, blocks, levels, chunk), out_shap...  44.5 us
    pallas_call x1, Pallas kernels, shards(): pl.pallas_call(functools.partial(write_out, pieces), out_shape=(jax.Shape...  1.67 us

profile of v7, /device:TPU:0, one launch (start us, length us, event | category | flops | bytes accessed | tf_op | source)
XLA Modules:
  0.0 46.8 jit_solution(11140240107243788755)
XLA Ops:
  0.6 44.5 %shard_map.86 = (bf16[576,512]{1,0:T(8,128)(2,1)S(1)}, f32[1,2,576,512]{3,2,1,0:T(8,128)S(1)}) custom-call(f32[3,1,1,512]{3,2,1,0:T(1,128)} %pos_hbm.1, f32[1,1,512]{2,1,0:T(1,128)} %area_hbm.1, s32[1,1,512]{2,1,0:T(1,128)} %order_hbm.1, bf16[576,512]{1,0:T(8,128)(2,1)} %bitcast.6, bf16[576,512]{1,0:T(8,128)(2,1)} %bitcast.7, bf16[512,512]{1,0:T(8,128)(2,1)} %bitcast.8, ...), custom_call_target="tpu_custom_call" | custom-call | tf_op jit(solution)/shard_map/pallas_call | solution.py:327
  45.2 1.7 %shard_map.87 = (bf16[576,512]{1,0:T(8,128)(2,1)}, f32[1,2,576,512]{3,2,1,0:T(8,128)}) custom-call(bf16[576,512]{1,0:T(8,128)(2,1)S(1)} %get-tuple-element.6.off, f32[1,2,576,512]{3,2,1,0:T(8,128)S(1)} %get-tuple-element.7.nested), custom_call_target="tpu_custom_call" | custom-call | tf_op jit(solution)/shard_map/pallas_call | solution.py:373

commit v8 on v6

--- a/solution.py
+++ b/solution.py
@@ -13,7 +13,7 @@
 
 
 def chunk_rows(share):
-    return max(rows for rows in range(8, min(share, 32) + 1, 8) if share % rows == 0)
+    return max(rows for rows in range(8, min(share, 24) + 1, 8) if share % rows == 0)
 
 
 def leaf_partner(me, level):
@@ -33,7 +33,7 @@
     count, panels = probe.shape
     share = count // blocks
     per_half = share // chunk
-    lag = 3
+    lag = 4
     total = 2 * per_half
     my_blk = lax.axis_index("blk")
     my_leaf = lax.axis_index("leaf")
@@ -218,7 +218,7 @@
                 start += size
         return found
 
-    probe_sizes, sketch_sizes = pieces([1, 2, 3]), pieces([3])
+    probe_sizes, sketch_sizes = pieces([1, 3, 4]), pieces([4])
 
     order_load.wait()
     places = lax.broadcasted_iota(jnp.int32, (panels, panels), 0)

time: 45 us -> 45.1 us (level)
  no operation moved by 1% of the time
where the time goes in v8:
time: 45.1 us; the launch traced here: 45 us
  Pallas kernels  44.3 us (98%)
  between operations  0.64 us (1%)
    pallas_call x1, Pallas kernels, shards(): pl.pallas_call(functools.partial(kernel, blocks, levels, chunk), out_shap...  42.7 us
    pallas_call x1, Pallas kernels, shards(): pl.pallas_call(functools.partial(write_out, pieces), out_shape=(jax.Shape...  1.67 us

profile of v8, /device:TPU:0, one launch (start us, length us, event | category | flops | bytes accessed | tf_op | source)
XLA Modules:
  0.0 45.0 jit_solution(7413626032674486778)
XLA Ops:
  0.6 42.7 %shard_map.86 = (bf16[576,512]{1,0:T(8,128)(2,1)S(1)}, f32[1,2,576,512]{3,2,1,0:T(8,128)S(1)}) custom-call(f32[3,1,1,512]{3,2,1,0:T(1,128)} %pos_hbm.1, f32[1,1,512]{2,1,0:T(1,128)} %area_hbm.1, s32[1,1,512]{2,1,0:T(1,128)} %order_hbm.1, bf16[576,512]{1,0:T(8,128)(2,1)} %bitcast.6, bf16[576,512]{1,0:T(8,128)(2,1)} %bitcast.7, bf16[512,512]{1,0:T(8,128)(2,1)} %bitcast.8, ...), custom_call_target="tpu_custom_call" | custom-call | tf_op jit(solution)/shard_map/pallas_call | solution.py:320
  43.3 1.7 %shard_map.87 = (bf16[576,512]{1,0:T(8,128)(2,1)}, f32[1,2,576,512]{3,2,1,0:T(8,128)}) custom-call(bf16[576,512]{1,0:T(8,128)(2,1)S(1)} %get-tuple-element.6.off, f32[1,2,576,512]{3,2,1,0:T(8,128)S(1)} %get-tuple-element.7.nested), custom_call_target="tpu_custom_call" | custom-call | tf_op jit(solution)/shard_map/pallas_call | solution.py:366
